TPU v7x, 512 devices: a whole 4x8x8 slice. The times are simulated.
512 devices in a mesh: grp: 2 (over x_lo), gene: 4 (over x_hi, core), cell: 64 (over z, y).
Axes of the slice: x: 4 (x_hi: 2, x_lo: 2; x = x_hi * 2 + x_lo), y: 8, z: 8, core: 2. Of those that a mesh axis runs over, the one named last changes fastest.
Arguments:
- data: bfloat16 [2, 15360, 16384], P('grp', 'gene', 'cell'), may hold values from 0 to 48
- shared_w: float32 [15360, 256], P(('gene', 'cell')), may hold values from 0.002 to 2
- specific_v: float32 [2, 15360, 256], P('grp', ('gene', 'cell')), may hold values from 0.0005 to 0.5
- factor_h: float32 [2, 256, 16384], P('grp', None, 'cell'), may hold values from 0.01 to 1
- cell_count: int32 [2], P('grp'), may hold values from 4096 to 16384, as said below
Outputs:
- new_w: float32 [15360, 256], P(('gene', 'cell'))
- new_v: float32 [2, 15360, 256], P('grp', ('gene', 'cell'))
- new_h: float32 [2, 256, 16384], P('grp', None, 'cell')
Inputs may be any that keep to these rules, and one draw needn't show every extreme that they name: `cell_count`: in each draw one dataset, chosen from the seed, has all 16384 cell slots live and the other between 4096 and 8192; the live slots are the first ones.
All inputs are finite; a program needn't handle non-finite values.
Results may differ from a plain program's by a relative error of at most 0.0044.
Values may be sent and summed in bfloat16 or wider, within the bound.
A program may use at most 64 MiB of HBM per device.

v0:
```python
import jax
import jax.numpy as jnp
from jax import lax
from jax.sharding import PartitionSpec as P

K = 256
KB = 32
SWEEPS = 4


LAMBDA = 5.0
TINY = 1e-06
HIGH = lax.Precision.HIGHEST


def side_by_side(arrays, axis, dim, along):
    widths = [a.shape[along] for a in arrays]
    both = jnp.concatenate(arrays, axis=along)
    out = lax.all_gather(both, axis, axis=dim, tiled=True)
    return tuple(jnp.split(out, [sum(widths[:k]) for k in range(1, len(widths))], axis=along))


def from_everyone(array, axis):
    copies = jnp.broadcast_to(array, (lax.axis_size(axis), *array.shape))
    return lax.all_to_all(copies, axis, split_axis=0, concat_axis=0, tiled=True)


def taken_together(array, axis):
    return from_everyone(array, axis).sum(axis=0)


def in_one(arrays, axis):
    line, at, done = (jnp.concatenate([a.reshape(-1) for a in arrays]), 0, [])
    so_far = taken_together(line, axis)
    for a in arrays:
        done.append(so_far[at : at + a.size].reshape(a.shape))
        at += a.size
    return tuple(done)


def split_up(array, dim, devices):
    dims = array.shape
    parts = array.reshape(*dims[:dim], devices, dims[dim] // devices, *dims[dim + 1 :])
    return jnp.moveaxis(parts, dim, 0)


def piece_ends(length, count):
    unit = 8 if length >= 8 * count else 1
    return [length // unit * k // count * unit for k in range(1, count)]


def in_order(parts, dim):
    dims = list(parts.shape[1:])
    dims[dim] *= parts.shape[0]
    return jnp.moveaxis(parts, 0, dim).reshape(dims)


def cut_exchange(array, axis, pieces, split_dim, concat_dim):
    parts = split_up(array, split_dim, lax.axis_size(axis))
    cut = max(range(1, max(2, parts.ndim - 1)), key=lambda d: parts.shape[d])
    done = []
    for slab in jnp.split(parts, piece_ends(parts.shape[cut], pieces), axis=cut):
        if slab.size:
            done.append(lax.all_to_all(slab, axis, split_axis=0, concat_axis=0, tiled=True))
    return in_order(jnp.concatenate(done, axis=cut), concat_dim)


def contract_rows(left, right):
    return lax.dot_general(
        left, right, (((0,), (0,)), ((), ())), preferred_element_type=jnp.float32
    )


def contract_cols(left, right):
    return lax.dot_general(
        left, right, (((1,), (1,)), ((), ())), preferred_element_type=jnp.float32
    )


def sweep_rows(state, gram, drive, live, width):

    def one(index, state):
        start = jnp.asarray(index).astype(jnp.int32) * width
        rows = lax.dynamic_slice_in_dim(gram, start, width, 0)
        grad = jnp.dot(rows, state, precision=HIGH) - lax.dynamic_slice_in_dim(
            drive, start, width, 0
        )
        block = lax.dynamic_slice_in_dim(rows, start, width, 1)
        scale = jnp.sum(jnp.abs(block), axis=1) + TINY
        current = lax.dynamic_slice_in_dim(state, start, width, 0)
        fresh = jnp.maximum(current - grad / scale[:, None], 0.0) * live[None, :]
        return lax.dynamic_update_slice_in_dim(state, fresh, start, 0)

    for sweep in range(SWEEPS):
        state = lax.fori_loop(0, K // width, one, state)
    return state


def sweep_columns(matrix, offset, quad, target, factor, width):

    def one(index, matrix):
        start = jnp.asarray(index).astype(jnp.int32) * width
        cols = lax.dynamic_slice_in_dim(quad, start, width, 1)
        grad = jnp.dot(factor * matrix + offset, cols, precision=HIGH) - lax.dynamic_slice_in_dim(
            target, start, width, 1
        )
        block = lax.dynamic_slice_in_dim(cols, start, width, 0)
        scale = factor * jnp.sum(jnp.abs(block), axis=0) + TINY
        current = lax.dynamic_slice_in_dim(matrix, start, width, 1)
        fresh = jnp.maximum(current - grad / scale[None, :], 0.0)
        return lax.dynamic_update_slice_in_dim(matrix, fresh, start, 1)

    for sweep in range(SWEEPS):
        matrix = lax.fori_loop(0, K // width, one, matrix)
    return matrix


def shards(data, shared_w, specific_v, factor_h, cell_count):
    expr = data[0]
    loading = specific_v[0]
    state = factor_h[0]
    cells = expr.shape[1]
    mix = (shared_w + loading).astype(jnp.bfloat16)
    own = loading.astype(jnp.bfloat16)
    part_mix, part_own = side_by_side((mix, own), "cell", 0, 1)
    drive = contract_rows(part_mix, expr)
    gram = contract_rows(part_mix, part_mix) + LAMBDA * contract_rows(part_own, part_own)
    drive, gram = (drive, gram)
    drive, gram = in_one((drive, gram), "gene")
    slots = lax.axis_index("cell") * cells + jnp.arange(cells, dtype=jnp.int32)
    live = (slots < cell_count[0]).astype(jnp.float32)
    state = sweep_rows(state, gram, drive, live, KB)
    rounded = state.astype(jnp.bfloat16)
    owned = cut_exchange(expr, "cell", 2, 0, 1)
    factors = lax.all_gather(rounded, "cell", axis=1, tiled=True)
    proj = contract_cols(owned, factors)
    cross = contract_cols(factors, factors)
    loading = sweep_columns(loading, shared_w, cross, proj, 1.0 + LAMBDA, KB)
    rest = proj - jnp.dot(loading, cross, precision=HIGH)
    rest, cross_sum = in_one((rest, cross), "grp")
    new_w = sweep_columns(
        shared_w, jnp.zeros(shared_w.shape, jnp.float32), cross_sum, rest, 1.0, KB
    )
    return (new_w, loading[None], state[None])


def solution(mesh):
    in_specs = (
        P("grp", "gene", "cell"),
        P(("gene", "cell"), None),
        P("grp", ("gene", "cell"), None),
        P("grp", None, "cell"),
        P("grp"),
    )
    out_specs = (
        P(("gene", "cell"), None),
        P("grp", ("gene", "cell"), None),
        P("grp", None, "cell"),
    )
    return jax.shard_map(shards, mesh=mesh, in_specs=in_specs, out_specs=out_specs, check_vma=False)
```

profile of v0, /device:TPU:1, one launch (start us, length us, event | category | flops | bytes accessed | tf_op | source)
XLA Modules:
  0.0 397.3 jit_solution(16595109983121796078)
XLA Ops:
  9.6 90.8 %all-gather.6.cloned.1.call-done = bf16[64,60,512]{2,1,0:T(8,128)(2,1)} async-done(((bf16[1,60,512]{2,1,0:T(8,128)(2,1)}), bf16[64,60,512]{2,1,0:T(8,128)(2,1)}) %all-gather.6.cloned.1.call-update) | async-done | bytes 3932176 | tf_op jit(solution)/shard_map/all_gather | solution.py:19
  100.4 6.3 %reshape.151 = bf16[3840,512]{1,0:T(8,128)(2,1)} reshape(bf16[64,60,512]{2,1,0:T(8,128)(2,1)} %all-gather.6.cloned.1.call-done) | data formatting | bytes 7864320
  106.7 3.0 fusion.102
  112.5 2.4 broadcast_in_dim.60
  114.9 8.8 %all-to-all-start.2 = ((f32[4,1,131072]{2,1,0:T(1,128)}), f32[4,1,131072]{2,1,0:T(1,128)S(1)}, u32[]{:S(2)}, u32[]{:S(2)}) async-start(f32[4,1,131072]{2,1,0:T(1,128)} %broadcast_in_dim.60), calls=%async_computation.2 | async-start | bytes 4194304 | tf_op jit(solution)/shard_map/all_to_all | solution.py:25
  123.7 26.3 %all-to-all-done.2 = f32[4,1,131072]{2,1,0:T(1,128)S(1)} async-done(((f32[4,1,131072]{2,1,0:T(1,128)}), f32[4,1,131072]{2,1,0:T(1,128)S(1)}, u32[]{:S(2)}, u32[]{:S(2)}) %all-to-all-start.2) | async-done | bytes 2097184 | tf_op jit(solution)/shard_map/all_to_all | solution.py:25
  150.0 1.9 reduce_sum.222
  152.2 9.2 %while.204 = (s32[]{:T(128)}, f32[256,256]{1,0:T(8,128)S(1)}, f32[256,256]{1,0:T(8,128)S(1)}, f32[256,256]{1,0:T(8,128)S(1)}, s32[]{:T(128)}, /*index=5*/s32[]{:...) while((s32[]{:T(128)}, f32[256,256]{1,0:T(8,128)S(1)}, ...), condition=%wide.region_3.0_spmd.clone, body=%wide.region_1.0_spmd.clone.sunk | while | flops 25209608 | bytes 467003 | solution.py:95
  161.4 9.2 %while.205 = (s32[]{:T(128)}, f32[256,256]{1,0:T(8,128)S(1)}, f32[256,256]{1,0:T(8,128)S(1)}, f32[256,256]{1,0:T(8,128)S(1)}, s32[]{:T(128)}, /*index=5*/s32[]{:...) while((s32[]{:T(128)}, f32[256,256]{1,0:T(8,128)S(1)}, ...), condition=%wide.region_6.0_spmd.clone, body=%wide.region_4.0_spmd.clone.sunk | while | flops 25209608 | bytes 467003 | solution.py:95
  170.6 9.2 %while.206 = (s32[]{:T(128)}, f32[256,256]{1,0:T(8,128)S(1)}, f32[256,256]{1,0:T(8,128)S(1)}, f32[256,256]{1,0:T(8,128)S(1)}, s32[]{:T(128)}, /*index=5*/s32[]{:...) while((s32[]{:T(128)}, f32[256,256]{1,0:T(8,128)S(1)}, ...), condition=%wide.region_9.0_spmd.clone, body=%wide.region_7.0_spmd.clone.sunk | while | flops 25209608 | bytes 467003 | solution.py:95
  179.8 9.2 %while.207 = (s32[]{:T(128)}, f32[256,256]{1,0:T(8,128)S(1)}, f32[256,256]{1,0:T(8,128)S(1)}, f32[256,256]{1,0:T(8,128)S(1)}, s32[]{:T(128)}, /*index=5*/s32[]{:...) while((s32[]{:T(128)}, f32[256,256]{1,0:T(8,128)S(1)}, ...), condition=%wide.region_12.0_spmd.clone, body=%wide.region_10.0_spmd.clone.sunk | while | flops 25209608 | bytes 467003 | solution.py:95
  189.8 2.4 reshape_squeeze.3
  193.2 8.4 %all-to-all-start = ((bf16[64,24,256]{2,1,0:T(8,128)(2,1)}), bf16[64,24,256]{2,1,0:T(8,128)(2,1)S(1)}, u32[]{:S(2)}, u32[]{:S(2)}) async-start(bf16[64,24,256]{2,1,0:T(8,128)(2,1)} %split.16), calls=%async_computation | async-start | bytes 1572864 | tf_op jit(solution)/shard_map/all_to_all | solution.py:64
  201.6 1.3 split.17
  202.9 22.9 %all-to-all-done = bf16[64,24,256]{2,1,0:T(8,128)(2,1)S(1)} async-done(((bf16[64,24,256]{2,1,0:T(8,128)(2,1)}), bf16[64,24,256]{2,1,0:T(8,128)(2,1)S(1)}, u32[]{:S(2)}, u32[]{:S(2)}) %all-to-all-start) | async-done | bytes 786464 | tf_op jit(solution)/shard_map/all_to_all | solution.py:64
  225.8 8.6 %all-to-all-start.1 = ((bf16[64,36,256]{2,1,0:T(8,128)(2,1)}), bf16[64,36,256]{2,1,0:T(8,128)(2,1)S(1)}, u32[]{:S(2)}, u32[]{:S(2)}) async-start(bf16[64,36,256]{2,1,0:T(8,128)(2,1)} %split.17), calls=%async_computation.1 | async-start | bytes 2621440 | tf_op jit(solution)/shard_map/all_to_all | solution.py:64
  234.7 32.2 %all-to-all-done.1 = bf16[64,36,256]{2,1,0:T(8,128)(2,1)S(1)} async-done(((bf16[64,36,256]{2,1,0:T(8,128)(2,1)}), bf16[64,36,256]{2,1,0:T(8,128)(2,1)S(1)}, u32[]{:S(2)}, u32[]{:S(2)}) %all-to-all-start.1) | async-done | bytes 1179680 | tf_op jit(solution)/shard_map/all_to_all | solution.py:64
  268.5 1.3 copy.102
  269.8 53.6 %all-gather.4.cloned.1.call-done = bf16[256,16384]{1,0:T(8,128)(2,1)} async-done(((bf16[256,256]{1,0:T(8,128)(2,1)}), bf16[256,16384]{1,0:T(8,128)(2,1)}) %all-gather.4.cloned.1.call-update) | async-done | bytes 8388624 | tf_op jit(solution)/shard_map/all_gather | solution.py:135
  323.4 6.0 %fusion.107 = f32[60,256]{1,0:T(8,128)S(1)} fusion(bf16[60,16384]{1,0:T(8,128)(2,1)S(1)} %bitcast.114, bf16[256,16384]{1,0:T(8,128)(2,1)} %all-gather.4.cloned.1.call-done), kind=kOutput, calls=%fused_computation.152 | convolution fusion | flops 503316480 | bytes 10416128 | tf_op jit(solution)/shard_map/dot_general | solution.py:75
  329.5 8.1 %fusion.108 = f32[256,256]{1,0:T(8,128)S(1)} fusion(bf16[256,16384]{1,0:T(8,128)(2,1)} %all-gather.4.cloned.1.call-done), kind=kOutput, calls=%fused_computation.153 | convolution fusion | flops 2147483648 | bytes 8650752 | tf_op jit(solution)/shard_map/dot_general | solution.py:75
  337.7 5.0 %while.196 = (s32[]{:T(128)}, f32[60,256]{0,1:T(8,128)S(1)}, f32[60,256]{0,1:T(8,128)S(1)}, f32[256,256]{1,0:T(8,128)S(1)}, f32[60,256]{0,1:T(8,128)S(1)}, /*ind...) while((s32[]{:T(128)}, f32[60,256]{0,1:T(8,128)S(1)}, f32[60,256]{0,1:T(8,128)S(1)}, ...), condition=%wide.region_15.0_spmd, body=%wide.region_13.0_spmd.sunk | while | flops 5938727 | bytes 571431 | solution.py:114
  342.6 5.0 %while.197 = (s32[]{:T(128)}, f32[60,256]{0,1:T(8,128)S(1)}, f32[60,256]{0,1:T(8,128)S(1)}, f32[256,256]{1,0:T(8,128)S(1)}, f32[60,256]{0,1:T(8,128)S(1)}, /*ind...) while((s32[]{:T(128)}, f32[60,256]{0,1:T(8,128)S(1)}, f32[60,256]{0,1:T(8,128)S(1)}, ...), condition=%wide.region_18.0_spmd, body=%wide.region_16.0_spmd.sunk | while | flops 5938727 | bytes 571431 | solution.py:114
  347.6 5.0 %while.198 = (s32[]{:T(128)}, f32[60,256]{0,1:T(8,128)S(1)}, f32[60,256]{0,1:T(8,128)S(1)}, f32[256,256]{1,0:T(8,128)S(1)}, f32[60,256]{0,1:T(8,128)S(1)}, /*ind...) while((s32[]{:T(128)}, f32[60,256]{0,1:T(8,128)S(1)}, f32[60,256]{0,1:T(8,128)S(1)}, ...), condition=%wide.region_21.0_spmd, body=%wide.region_19.0_spmd.sunk | while | flops 5938727 | bytes 571431 | solution.py:114
  352.6 5.0 %while.199 = (s32[]{:T(128)}, f32[60,256]{0,1:T(8,128)S(1)}, f32[60,256]{0,1:T(8,128)S(1)}, f32[256,256]{1,0:T(8,128)S(1)}, f32[60,256]{0,1:T(8,128)S(1)}, /*ind...) while((s32[]{:T(128)}, f32[60,256]{0,1:T(8,128)S(1)}, f32[60,256]{0,1:T(8,128)S(1)}, ...), condition=%wide.region_24.0_spmd, body=%wide.region_22.0_spmd.sunk | while | flops 5938727 | bytes 571431 | solution.py:114
  358.1 1.2 broadcast_in_dim.61
  359.3 3.5 all-to-all-start.3
  363.5 5.4 %all-to-all-done.3 = f32[2,1,80896]{2,1,0:T(1,128)S(1)} async-done(((f32[2,1,80896]{2,1,0:T(1,128)}), f32[2,1,80896]{2,1,0:T(1,128)S(1)}, u32[]{:S(2)}, u32[]{:S(2)}) %all-to-all-start.3) | async-done | bytes 647200 | tf_op jit(solution)/shard_map/all_to_all | solution.py:25
  370.0 4.9 %while.200 = (s32[]{:T(128)}, f32[60,256]{0,1:T(8,128)S(1)}, f32[256,256]{1,0:T(8,128)S(1)}, f32[60,256]{0,1:T(8,128)S(1)}, s32[]{:T(128)}, /*index=5*/s32[]{:T(128)}, s32[]{:T(128)}, s32[]{:T(128)}, s32[]{:T(128)}) while((s32[]{:T(128)}, f32[60,256]{0,1:T(8,128)S(1)}, f32[256,256]{1,0:T(8,128)S(1)}, f32[60,256]{0,1:T(8,128)S(1)}, ...), condition=%wide.region_28.0_spmd, body=%wide.region_26.0_spmd.sunk | while | flops 5907975 | bytes 341539 | solution.py:114
  375.0 4.9 %while.201 = (s32[]{:T(128)}, f32[60,256]{0,1:T(8,128)S(1)}, f32[256,256]{1,0:T(8,128)S(1)}, f32[60,256]{0,1:T(8,128)S(1)}, s32[]{:T(128)}, /*index=5*/s32[]{:T(128)}, s32[]{:T(128)}, s32[]{:T(128)}, s32[]{:T(128)}) while((s32[]{:T(128)}, f32[60,256]{0,1:T(8,128)S(1)}, f32[256,256]{1,0:T(8,128)S(1)}, f32[60,256]{0,1:T(8,128)S(1)}, ...), condition=%wide.region_31.0_spmd, body=%wide.region_29.0_spmd.sunk | while | flops 5907975 | bytes 341539 | solution.py:114
  379.9 4.9 %while.202 = (s32[]{:T(128)}, f32[60,256]{0,1:T(8,128)S(1)}, f32[256,256]{1,0:T(8,128)S(1)}, f32[60,256]{0,1:T(8,128)S(1)}, s32[]{:T(128)}, /*index=5*/s32[]{:T(128)}, s32[]{:T(128)}, s32[]{:T(128)}, s32[]{:T(128)}) while((s32[]{:T(128)}, f32[60,256]{0,1:T(8,128)S(1)}, f32[256,256]{1,0:T(8,128)S(1)}, f32[60,256]{0,1:T(8,128)S(1)}, ...), condition=%wide.region_34.0_spmd, body=%wide.region_32.0_spmd.sunk | while | flops 5907975 | bytes 341539 | solution.py:114
  384.8 4.9 %while.203 = (s32[]{:T(128)}, f32[60,256]{0,1:T(8,128)S(1)}, f32[256,256]{1,0:T(8,128)S(1)}, f32[60,256]{0,1:T(8,128)S(1)}, s32[]{:T(128)}, /*index=5*/s32[]{:T(128)}, s32[]{:T(128)}, s32[]{:T(128)}, s32[]{:T(128)}) while((s32[]{:T(128)}, f32[60,256]{0,1:T(8,128)S(1)}, f32[256,256]{1,0:T(8,128)S(1)}, f32[60,256]{0,1:T(8,128)S(1)}, ...), condition=%wide.region_37.0_spmd, body=%wide.region_35.0_spmd.sunk | while | flops 5907975 | bytes 341539 | solution.py:114
  (463 shorter events, 84.7 us)
Async XLA Ops:
  7.2 93.2 %all-gather.6.cloned.1.call-start = ((), (), s32[]{:S(2)}) async-start(), calls=%async_computation.5 | async-start | bytes 4259840 | tf_op jit(solution)/shard_map/all_gather | solution.py:19
  106.7 3.3 copy-start.2
  110.0 1.5 copy-start.3
  114.9 35.1 %all-to-all-start.2 = ((f32[4,1,131072]{2,1,0:T(1,128)}), f32[4,1,131072]{2,1,0:T(1,128)S(1)}, u32[]{:S(2)}, u32[]{:S(2)}) async-start(f32[4,1,131072]{2,1,0:T(1,128)} %broadcast_in_dim.60), calls=%async_computation.2 | async-start | bytes 4194304 | tf_op jit(solution)/shard_map/all_to_all | solution.py:25
  123.7 199.7 %all-gather.4.cloned.1.call-start = ((), (), s32[]{:S(2)}) async-start(), calls=%async_computation.4 | async-start | bytes 8519680 | tf_op jit(solution)/shard_map/all_gather | solution.py:135
  123.7 28.5 %copy-start.1 = (f32[1,256,256]{2,1,0:T(8,128)S(1)}, f32[1,256,256]{2,1,0:T(8,128)}, u32[]{:S(2)}) copy-start(f32[1,256,256]{2,1,0:T(8,128)} %param.32) | copy-start | bytes 786436
  189.0 3.2 copy-start
  193.2 32.6 %all-to-all-start = ((bf16[64,24,256]{2,1,0:T(8,128)(2,1)}), bf16[64,24,256]{2,1,0:T(8,128)(2,1)S(1)}, u32[]{:S(2)}, u32[]{:S(2)}) async-start(bf16[64,24,256]{2,1,0:T(8,128)(2,1)} %split.16), calls=%async_computation | async-start | bytes 1572864 | tf_op jit(solution)/shard_map/all_to_all | solution.py:64
  201.6 32.8 %copy-start.5 = (f32[60,256]{1,0:T(8,128)S(1)}, f32[60,256]{1,0:T(8,128)}, u32[]{:S(2)}) copy-start(f32[60,256]{1,0:T(8,128)} %param.30) | copy-start | bytes 184324
  201.6 32.9 %copy-start.4 = (f32[1,60,256]{2,0,1:T(1,128)S(1)}, f32[1,60,256]{2,0,1:T(1,128)}, u32[]{:S(2)}) copy-start(f32[1,60,256]{2,0,1:T(1,128)} %param.31) | copy-start | bytes 184324
  225.8 41.1 %all-to-all-start.1 = ((bf16[64,36,256]{2,1,0:T(8,128)(2,1)}), bf16[64,36,256]{2,1,0:T(8,128)(2,1)S(1)}, u32[]{:S(2)}, u32[]{:S(2)}) async-start(bf16[64,36,256]{2,1,0:T(8,128)(2,1)} %split.17), calls=%async_computation.1 | async-start | bytes 2621440 | tf_op jit(solution)/shard_map/all_to_all | solution.py:64
  359.3 9.6 %all-to-all-start.3 = ((f32[2,1,80896]{2,1,0:T(1,128)}), f32[2,1,80896]{2,1,0:T(1,128)S(1)}, u32[]{:S(2)}, u32[]{:S(2)}) async-start(f32[2,1,80896]{2,1,0:T(1,128)} %broadcast_in_dim.61), calls=%async_computation.3 | async-start | bytes 1294336 | tf_op jit(solution)/shard_map/all_to_all | solution.py:25
Sparse Core Ops, SparseCore 0:
  11.6 88.7 all-gather.5
  189.9 133.4 all-gather.3
where the time goes:
time: 402 us; the launch traced here: 397 us
  waiting for transfers between devices  231 us (57%)
  matrix products  56.6 us (14%)
  other arithmetic  39.7 us (10%)
  starting transfers between devices  29.4 us (7%)
  local copies, waits for them, and re-layouts  22.3 us (6%)
  between operations  14.4 us (4%)
    all_gather x1, waiting for transfers between devices, side_by_side(): out = lax.all_gather(both, axis, axis=dim, tiled=True)  90.8 us
    all_to_all x2, waiting for transfers between devices, cut_exchange(): lax.all_to_all(slab, axis, split_axis=0, concat_axis=0, tiled=True)  55.1 us
    all_gather x1, waiting for transfers between devices, shards(): factors = lax.all_gather(rounded, 'cell', axis=1, tiled=True)  53.6 us
    all_to_all x2, waiting for transfers between devices, from_everyone(): return lax.all_to_all(copies, axis, split_axis=0, concat_axis=0, tiled=True)  31.7 us
    dot_general x64, matrix products, one(): jnp.dot(factor * matrix + offset, cols, precision=HIGH)  29.9 us
    convert_element_type x32, other arithmetic, shards(): live = (slots < cell_count[0]).astype(jnp.float32)  20.9 us
    all_to_all x2, starting transfers between devices, cut_exchange(): lax.all_to_all(slab, axis, split_axis=0, concat_axis=0, tiled=True)  17.1 us
    dot_general x2, matrix products, contract_cols(): lax.dot_general(left, right, (((1,), (1,)), ((), ())), preferred_element_...  14.2 us
  transfers between devices with their start and end apart: 6, of which 6 were waited for; matrix products, arithmetic and copies ran while one was open for 2% of the time, Pallas kernels for 0%

commit v1 on v0

v1 whole, which is shorter than its diff:
```python
import jax
import jax.numpy as jnp
from jax import lax
from jax.experimental import pallas as pl
from jax.experimental.pallas import tpu as pltpu
from jax.sharding import PartitionSpec as P

K = 256
KB = 32
SWEEPS = 4
LAMBDA = 5.0
TINY = 1e-06
N = 8
GENES = 4
OWN = 60
ROWS = 64
HALF = 32
F32 = jnp.float32
BF16 = jnp.bfloat16
MESH = pl.DeviceIdType.MESH


def dot(left, right, left_dim=1, right_dim=0):
    return lax.dot_general(
        left, right, (((left_dim,), (right_dim,)), ((), ())), preferred_element_type=F32
    )


def split(x):
    high = x.astype(BF16)
    return high, (x - high.astype(F32)).astype(BF16)


def dot_split(left, high, low):
    one, two = split(left)
    return dot(one, high) + (dot(two, high) + dot(one, low))


def block_scale(quad):
    row = lax.broadcasted_iota(jnp.int32, (K, K), 0) // KB
    col = lax.broadcasted_iota(jnp.int32, (K, K), 1) // KB
    return jnp.sum(jnp.where(row == col, jnp.abs(quad), 0.0), axis=0, keepdims=True)


def sweeps(state, resid, quads, inverse, factor, live):
    lane = lax.broadcasted_iota(jnp.int32, (ROWS, 128), 1) // KB

    def one(_, carry):
        halves, resid = list(carry[:2]), carry[2]
        for block in range(K // KB):
            at = block // 4
            lanes = slice(at * 128, at * 128 + 128)
            now = halves[at]
            fresh = jnp.maximum(now - resid[:, lanes] * inverse[:, lanes], 0.0)
            if live is not None:
                fresh = fresh * live
            fresh = jnp.where(lane == block % 4, fresh, now)
            change = fresh - now
            if factor != 1.0:
                change = change * factor
            halves[at] = fresh
            both = jnp.concatenate(split(change), axis=1)
            resid = resid + (dot(both, quads[at]) + dot(both, quads[2 + at]))
        return halves[0], halves[1], resid

    first, second, _ = lax.fori_loop(
        0, SWEEPS, one, (state[:, :128], state[:, 128:], resid)
    )
    return jnp.concatenate([first, second], axis=1)


def kernel(
    count_ref, expr_hbm, w_ref, v_ref, h_ref,
    new_w_ref, new_v_ref, new_h_ref,
    expr, ea, eb, et, ma, mb, acc, wp, vp, ht, hb,
    gp, g1, gr, g2, g3, g4, gram,
    dr, pa, pb, ring, qa, qb, cp_, c2, cr, c3, c4, cross,
    rest, rest_in, cross_in, quads,
    local_sem, s1s, s1r, ags, agr, gs, gr_s, hs, hr, rs, rr, qs, qr, zs, zr,
):
    c = lax.axis_index("cell")
    g = lax.axis_index("gene")
    grp = lax.axis_index("grp")
    z, y = c // N, c % N

    def plus(a, k):
        return lax.rem(a + (k + N), N)

    def at_z(k):
        return {"cell": plus(z, k) * N + y}

    def at_y(k):
        return {"cell": z * N + plus(y, k)}

    def at_gene(k):
        return {"gene": lax.rem(g + k, GENES)}

    other = {"grp": 1 - grp}
    started = []

    def send(src, dst, send_sem, recv_sem, device):
        copy = pltpu.make_async_remote_copy(
            src_ref=src, dst_ref=dst, send_sem=send_sem, recv_sem=recv_sem,
            device_id=device, device_id_type=MESH,
        )
        copy.start()
        started.append(copy)
        return copy

    load = pltpu.make_async_copy(expr_hbm, expr, local_sem)
    load.start()

    barrier = pltpu.get_barrier_semaphore()
    for k in range(1, N):
        pl.semaphore_signal(barrier, inc=1, device_id=at_z(k), device_id_type=MESH)
        pl.semaphore_signal(barrier, inc=1, device_id=at_y(k), device_id_type=MESH)
    for k in range(1, GENES):
        pl.semaphore_signal(barrier, inc=1, device_id=at_gene(k), device_id_type=MESH)
    pl.semaphore_signal(barrier, inc=1, device_id=other, device_id_type=MESH)

    wp[...] = jnp.zeros_like(wp)
    vp[...] = jnp.zeros_like(vp)
    wp[0:OWN, :] = w_ref[...]
    vp[0:OWN, :] = v_ref[...]
    mix = (wp[...] + vp[...]).astype(BF16)
    own = vp[...].astype(BF16)
    ht[...] = h_ref[...].T
    ma[z, y] = mix[:HALF]
    mb[y, z] = mix[HALF:]
    gp[...] = dot(mix, mix, 0, 0) + LAMBDA * dot(own, own, 0, 0)

    pl.semaphore_wait(barrier, 2 * (N - 1) + GENES)

    order = [4, 3, 5, 2, 6, 1, 7]
    first = []
    for k in order:
        first.append(send(ma.at[z, y], ma.at[z, y], s1s.at[0, k], s1r.at[0, k], at_y(k)))
        first.append(send(mb.at[y, z], mb.at[y, z], s1s.at[1, k], s1r.at[1, k], at_z(k)))

    def scatter_gene(src, into, row):
        done = []
        for k in range(1, GENES):
            to = lax.rem(g + k, GENES)
            rows = pl.ds(pl.multiple_of(to * ROWS, ROWS), ROWS)
            done.append(send(src.at[rows], into.at[k], gs.at[row, k], gr_s.at[row, k], at_gene(k)))
        return done

    def gather_gene(ref, size, row, sems, sems_r):
        rows = pl.ds(pl.multiple_of(g * size, size), size)
        return [
            send(ref.at[rows], ref.at[rows], sems.at[row, k], sems_r.at[row, k], at_gene(k))
            for k in range(1, GENES)
        ]

    def landed(copies):
        for copy in copies:
            copy.wait_recv()

    my_rows = pl.ds(pl.multiple_of(g * ROWS, ROWS), ROWS)
    my_eight = pl.ds(pl.multiple_of(z * 8, 8), 8)

    def reduce_z(part, into, row):
        done = []
        for k in range(1, N):
            rows = pl.ds(pl.multiple_of(plus(z, k) * 8, 8), 8)
            done.append(send(part.at[rows], into.at[k], zs.at[row, k], zr.at[row, k], at_z(k)))
        return done

    def share_y(part, into, row):
        return [
            send(part, into.at[k], zs.at[row, k], zr.at[row, k], at_y(k)) for k in range(1, N)
        ]

    def gather_z(ref, row):
        return [
            send(
                ref.at[pl.ds(pl.multiple_of(g * ROWS + z * 8, 8), 8)],
                ref.at[pl.ds(pl.multiple_of(g * ROWS + z * 8, 8), 8)],
                zs.at[row, k], zr.at[row, k], at_z(k),
            )
            for k in range(1, N)
        ]

    gram_one = scatter_gene(gp, g1, 0)

    load.wait()

    def lay_out(four, carry):
        part = expr[pl.ds(pl.multiple_of(four * 240, 16), 240), :]
        for k in range(4):
            owner = four * 4 + k
            oz, oy = owner // N, owner % N
            ea[oz, oy] = part[k * OWN : k * OWN + HALF]
            tail = jnp.concatenate(
                [part[k * OWN + HALF : (k + 1) * OWN].astype(F32), jnp.zeros((ROWS - OWN, K), F32)],
                axis=0,
            )
            eb[oy, oz] = tail.astype(BF16)
        return carry

    lax.fori_loop(0, 16, lay_out, 0)

    landed(first)

    ring_ag = {}

    def ag_send(step):
        for sub in range(2):
            for d in (0, 1):
                if step == N // 2 and sub != d:
                    continue
                sign = 1 - 2 * d
                for axis in (0, 1):
                    if step > 1:
                        ring_ag[axis, d, step - 1, sub].wait_recv()
                    if axis == 0:
                        ref = ma.at[plus(z, -sign * (step - 1)), pl.ds(sub * 4, 4)]
                        device = at_z(sign)
                    else:
                        ref = mb.at[plus(y, -sign * (step - 1)), pl.ds(sub * 4, 4)]
                        device = at_y(sign)
                    ring_ag[axis, d, step, sub] = send(
                        ref, ref, ags.at[axis, d, step, sub], agr.at[axis, d, step, sub], device
                    )

    def ag_rest(step):
        for (axis, d, s, sub), copy in ring_ag.items():
            if s == step and (step == N // 2 or (step == N // 2 - 1 and sub != d)):
                copy.wait_recv()

    def chunk_of(ref, index):
        return ref[index].reshape(K, K)

    def drive_part(shifts, fresh=False):
        total = None
        for k in shifts:
            term = dot(chunk_of(et.at[0], plus(z, k)), chunk_of(ma, plus(z, k)))
            term = term + dot(chunk_of(et.at[1], plus(y, k)), chunk_of(mb, plus(y, k)))
            total = term if total is None else total + term
        acc[...] = total if fresh else acc[...] + total

    ag_send(1)

    def turn(k, carry):
        et[0, k] = ea[k].reshape(K, K).T
        et[1, k] = eb[k].reshape(K, K).T
        return carry

    lax.fori_loop(0, N, turn, 0)

    landed(gram_one)
    gr[...] = gp[my_rows, :] + (g1[1] + g1[2] + g1[3])
    gram_two = reduce_z(gr, g2, 0)
    drive_part([0], True)
    ag_send(2)
    landed(gram_two)
    total = gr[my_eight, :]
    for k in range(1, N):
        total = total + g2[k]
    g4[...] = total
    gram_three = share_y(g4, g3, 1)
    drive_part([-1, 1])
    ag_send(3)
    landed(gram_three)
    total = g4[...]
    for k in range(1, N):
        total = total + g3[k]
    gram[pl.ds(pl.multiple_of(g * ROWS + z * 8, 8), 8), :] = total
    gram_four = gather_z(gram, 2)
    drive_part([-2, 2])
    ag_send(4)
    landed(gram_four)
    gram_five = gather_gene(gram, ROWS, 1, gs, gr_s)
    ag_rest(3)
    drive_part([-3, 3])
    ag_rest(4)
    drive_part([4])
    drive_out = scatter_gene(acc, dr, 2)

    landed(gram_five)

    def stage_quad(quad):
        high, low = split(quad)
        for half in (0, 1):
            lanes = slice(half * 128, half * 128 + 128)
            for k in (0, 1):
                rows = slice(k * 128, k * 128 + 128)
                quads[half, rows, :] = high[lanes]
                quads[2 + half, rows, :] = low[lanes]
        return high, low

    state = ht[my_rows, :]
    high, low = stage_quad(gram[...])
    inverse = 1.0 / (block_scale(gram[...]) + TINY)
    resid = dot_split(state, high, low)
    slot = c * K + g * ROWS + lax.broadcasted_iota(jnp.int32, (ROWS, 128), 0)
    live = jnp.where(slot < count_ref[0], 1.0, 0.0).astype(F32)
    landed(drive_out)
    resid = resid - (acc[my_rows, :] + (dr[1] + dr[2] + dr[3]))
    state = sweeps(state, resid, quads, inverse, 1.0, live)
    ht[my_rows, :] = state
    hb[my_rows, :] = state.astype(BF16)
    hb_out = gather_gene(hb, ROWS, 0, hs, hr)
    h_out = gather_gene(ht, ROWS, 1, hs, hr)
    landed(hb_out)

    rings = {}

    def project(k):
        zk, yk = plus(z, k), plus(y, k)
        pa[zk] = dot(chunk_of(ea, zk), hb[...]).reshape(N, HALF, K)
        pb[yk] = dot(chunk_of(eb, yk), hb[...]).reshape(N, HALF, K)

    def rs_send(step):
        for sub in range(2):
            part = pl.ds(sub * 4, 4)
            for d in (0, 1):
                if step == 1 and sub != d:
                    continue
                sign = 1 - 2 * d
                for axis in (0, 1):
                    to = sign * (N // 2 + 1 - step)
                    if axis == 0:
                        mine, device = pa.at[plus(z, to), part], at_z(sign)
                    else:
                        mine, device = pb.at[plus(y, to), part], at_y(sign)
                    if step > 1 and (axis, d, step - 1, sub) in rings:
                        rings[axis, d, step - 1, sub].wait_recv()
                        here = ring.at[axis, d, step - 1, part]
                        here[...] = here[...] + mine[...]
                        mine = here
                    rings[axis, d, step, sub] = send(
                        mine, ring.at[axis, d, step, part],
                        rs.at[axis, d, step, sub], rr.at[axis, d, step, sub], device,
                    )

    project(4)
    rs_send(1)
    cp_[...] = dot(hb[...], hb[...], 0, 0)
    cr[...] = cp_[my_rows, :]
    cross_two = reduce_z(cr, c2, 3)
    project(3)
    project(-3)
    rs_send(2)
    landed(cross_two)
    total = cr[my_eight, :]
    for k in range(1, N):
        total = total + c2[k]
    c4[...] = total
    cross_three = share_y(c4, c3, 4)
    project(2)
    project(-2)
    rs_send(3)
    landed(cross_three)
    total = c4[...]
    for k in range(1, N):
        total = total + c3[k]
    cross[pl.ds(pl.multiple_of(g * ROWS + z * 8, 8), 8), :] = total
    cross_four = gather_z(cross, 5)
    project(1)
    project(-1)
    rs_send(4)
    landed(cross_four)
    cross_five = gather_gene(cross, ROWS, 3, gs, gr_s)
    project(0)
    landed(h_out)
    new_h_ref[...] = ht[...].T
    landed(cross_five)
    cross_other = send(cross, cross_in, gs.at[4, 0], gr_s.at[4, 0], other)
    high, low = stage_quad(cross[...])
    scale = block_scale(cross[...])
    resid = dot_split((1.0 + LAMBDA) * vp[...] + wp[...], high, low)
    for sub in range(2):
        part = pl.ds(sub * 4, 4)
        for axis in (0, 1):
            for d in (0, 1):
                rings[axis, d, 4, sub].wait_recv()
            mine = pa.at[z, part] if axis == 0 else pb.at[y, part]
            mine[...] = mine[...] + (ring[axis, 0, 4, part] + ring[axis, 1, 4, part])
    last = []
    for k in order:
        last.append(send(pa.at[z, plus(y, k)], qa.at[k], qs.at[0, k], qr.at[0, k], at_y(k)))
        last.append(send(pb.at[y, plus(z, k)], qb.at[k], qs.at[1, k], qr.at[1, k], at_z(k)))
    landed(last)
    one, two = pa[z, y], pb[y, z]
    for k in range(1, N):
        one = one + qa[k]
        two = two + qb[k]
    proj = jnp.concatenate([one, two], axis=0)

    state = sweeps(
        vp[...], resid - proj, quads, 1.0 / ((1.0 + LAMBDA) * scale + TINY), 1.0 + LAMBDA, None
    )
    vp[...] = state
    rest[...] = proj - dot_split(state, high, low)
    rest_other = send(rest, rest_in, gs.at[4, 1], gr_s.at[4, 1], other)
    new_v_ref[...] = vp[0:OWN, :]
    landed([cross_other])
    both = cross[...] + cross_in[...]
    high, low = stage_quad(both)
    scale = block_scale(both)
    resid = dot_split(wp[...], high, low)
    landed([rest_other])
    resid = resid - (rest[...] + rest_in[...])
    wp[...] = sweeps(wp[...], resid, quads, 1.0 / (scale + TINY), 1.0, None)
    new_w_ref[...] = wp[0:OWN, :]
    for copy in started:
        copy.wait_send()


def shards(data, shared_w, specific_v, factor_h, cell_count):
    vmem = pl.BlockSpec(memory_space=pltpu.VMEM)
    sems = pltpu.SemaphoreType.DMA
    new_w, new_v, new_h = pl.pallas_call(
        kernel,
        out_shape=(
            jax.ShapeDtypeStruct((OWN, K), F32),
            jax.ShapeDtypeStruct((OWN, K), F32),
            jax.ShapeDtypeStruct((K, K), F32),
        ),
        in_specs=[
            pl.BlockSpec(memory_space=pltpu.SMEM),
            pl.BlockSpec(memory_space=pl.ANY),
            vmem, vmem, vmem,
        ],
        out_specs=(vmem, vmem, vmem),
        scratch_shapes=[
            pltpu.VMEM((N * N * OWN, K), BF16),
            pltpu.VMEM((N, N, HALF, K), BF16),
            pltpu.VMEM((N, N, HALF, K), BF16),
            pltpu.VMEM((2, N, K, K), BF16),
            pltpu.VMEM((N, N, HALF, K), BF16),
            pltpu.VMEM((N, N, HALF, K), BF16),
            pltpu.VMEM((K, K), F32),
            pltpu.VMEM((ROWS, K), F32),
            pltpu.VMEM((ROWS, K), F32),
            pltpu.VMEM((K, K), F32),
            pltpu.VMEM((K, K), BF16),
            pltpu.VMEM((K, K), F32),
            pltpu.VMEM((GENES, ROWS, K), F32),
            pltpu.VMEM((ROWS, K), F32),
            pltpu.VMEM((N, 8, K), F32),
            pltpu.VMEM((N, 8, K), F32),
            pltpu.VMEM((8, K), F32),
            pltpu.VMEM((K, K), F32),
            pltpu.VMEM((GENES, ROWS, K), F32),
            pltpu.VMEM((N, N, HALF, K), F32),
            pltpu.VMEM((N, N, HALF, K), F32),
            pltpu.VMEM((2, 2, 5, N, HALF, K), F32),
            pltpu.VMEM((N, HALF, K), F32),
            pltpu.VMEM((N, HALF, K), F32),
            pltpu.VMEM((K, K), F32),
            pltpu.VMEM((N, 8, K), F32),
            pltpu.VMEM((ROWS, K), F32),
            pltpu.VMEM((N, 8, K), F32),
            pltpu.VMEM((8, K), F32),
            pltpu.VMEM((K, K), F32),
            pltpu.VMEM((ROWS, K), F32),
            pltpu.VMEM((ROWS, K), F32),
            pltpu.VMEM((K, K), F32),
            pltpu.VMEM((4, K, K), BF16),
            sems,
            sems((2, N)), sems((2, N)),
            sems((2, 2, 5, 2)), sems((2, 2, 5, 2)),
            sems((5, GENES)), sems((5, GENES)),
            sems((2, GENES)), sems((2, GENES)),
            sems((2, 2, 5, 2)), sems((2, 2, 5, 2)),
            sems((2, N)), sems((2, N)),
            sems((6, N)), sems((6, N)),
        ],
        compiler_params=pltpu.CompilerParams(
            collective_id=0, has_side_effects=True, vmem_limit_bytes=48 << 20
        ),
        cost_estimate=pl.CostEstimate(
            flops=1200000000, bytes_accessed=4000000, transcendentals=0
        ),
    )(cell_count, data[0], shared_w, specific_v[0], factor_h[0])
    return new_w, new_v[None], new_h[None]


def solution(mesh):
    in_specs = (
        P("grp", "gene", "cell"),
        P(("gene", "cell"), None),
        P("grp", ("gene", "cell"), None),
        P("grp", None, "cell"),
        P("grp"),
    )
    out_specs = (
        P(("gene", "cell"), None),
        P("grp", ("gene", "cell"), None),
        P("grp", None, "cell"),
    )
    return jax.shard_map(shards, mesh=mesh, in_specs=in_specs, out_specs=out_specs, check_vma=False)
```

time: 402 us -> 114 us (0.28); the launches traced: 397 us -> 114 us
  waiting for transfers between devices: 231 us -> 0 us
  Pallas kernels: 0 us -> 107 us
  matrix products: 56.6 us -> 0 us
  other arithmetic: 39.7 us -> 0 us
  starting transfers between devices: 29.4 us -> 0 us
  local copies, waits for them, and re-layouts: 22.3 us -> 6.19 us
  between operations: 14.4 us -> 1.29 us
    all_gather x2 -> x0, waiting for transfers between devices: 144 us -> none  [the longest x1 90.8 us: side_by_side(): out = lax.all_gather(both, axis, axis=dim, tiled=True)]
    pallas_call x0 -> x1, Pallas kernels: none -> 107 us  [shards(): pl.pallas_call(kernel, out_shape=(jax.ShapeDtypeStruct((OWN, K), F32), ja...]
    all_to_all x4 -> x0, waiting for transfers between devices: 86.8 us -> none  [the longest x2 55.1 us: cut_exchange(): lax.all_to_all(slab, axis, split_axis=0, concat_axis=0, tiled=True)]
    dot_general x102 -> x0, matrix products: 56.6 us -> none  [the longest x64 29.9 us: one(): jnp.dot(factor * matrix + offset, cols, precision=HIGH)]
    all_to_all x4 -> x0, starting transfers between devices: 29.4 us -> none  [the longest x2 17.1 us: cut_exchange(): lax.all_to_all(slab, axis, split_axis=0, concat_axis=0, tiled=True)]
    convert_element_type x34 -> x0, other arithmetic: 22.5 us -> none  [the longest x32 20.9 us: shards(): live = (slots < cell_count[0]).astype(jnp.float32)]
    reduce_sum x98 -> x0, other arithmetic: 15.3 us -> none  [the longest x64 6.43 us: one(): scale = factor * jnp.sum(jnp.abs(block), axis=0) + TINY]
    unnamed x21 -> x10, local copies, waits for them, and re-layouts: 10.9 us -> 6.19 us
  transfers between devices with their start and end apart: 6 -> 0, of which waited for: 6 -> 0; matrix products, arithmetic and copies ran while one was open for 2% -> 0% of each run, Pallas kernels for 0% -> 0%
where the time goes in v1:
time: 114 us
  Pallas kernels  107 us (94%)
  local copies, waits for them, and re-layouts  6.19 us (5%)
  between operations  1.29 us (1%)
    pallas_call x1, Pallas kernels, shards(): pl.pallas_call(kernel, out_shape=(jax.ShapeDtypeStruct((OWN, K), F32), ja...  107 us
    unnamed x10, local copies, waits for them, and re-layouts  6.19 us

profile of v1, /device:TPU:1, one launch (start us, length us, event | category | flops | bytes accessed | tf_op | source)
XLA Modules:
  0.0 114.1 jit_solution(4029534790760998113)
XLA Ops:
  1.3 0.8 copy.11
  2.1 0.0 copy-start
  2.1 1.5 %copy-done = bf16[1,3840,256]{2,1,0:T(8,128)(2,1)S(1)} copy-done((bf16[1,3840,256]{2,1,0:T(8,128)(2,1)S(1)}, bf16[1,3840,256]{2,1,0:T(8,128)(2,1)}, u32[]{:S(2)}) %copy-start) | copy-done | bytes 1966104
  3.7 0.0 copy-start.1
  3.7 0.9 copy-done.1
  4.6 0.0 copy-start.2
  4.6 0.8 copy-done.2
  5.4 106.6 %shard_map.76 = (f32[60,256]{1,0:T(8,128)S(1)}, f32[60,256]{1,0:T(8,128)S(1)}, f32[256,256]{1,0:T(8,128)S(1)}) custom-call(s32[1]{0:T(128)S(6)} %copy.14.count_ref, bf16[3840,256]{1,0:T(8,128)(2,1)S(1)} %bitcast.10, f32[60,256]{1,0:T(8,128)S(1)} %copy-done.2, f32[60,256]{1,0:T(8,128)S(1)} %bitcast.9, f32[256,256]{1,0:T(8,128)S(1)} %bitcast.11), custom_call_target="tpu_custom_call" | custom-call | flops 1200000000 | bytes 4000000 | tf_op jit(solution)/shard_map/pallas_call | solution.py:414
  112.1 0.7 copy.8
  112.8 0.6 copy.15
  113.4 0.7 copy.16
Async XLA Ops:
  2.1 1.5 %copy-start = (bf16[1,3840,256]{2,1,0:T(8,128)(2,1)S(1)}, bf16[1,3840,256]{2,1,0:T(8,128)(2,1)}, u32[]{:S(2)}) copy-start(bf16[1,3840,256]{2,1,0:T(8,128)(2,1)} %param.5) | copy-start | bytes 5898244
  3.7 0.9 copy-start.1
  4.6 0.8 copy-start.2
